TPU v7x, 32 devices: a whole 2x2x4 slice. The times are simulated.
32 devices in a mesh: groups: 1, expert: 16 (over z, y, x), tower: 2 (over core).
Axes of the slice: x: 2, y: 2, z: 4, core: 2. Of those that a mesh axis runs over, the one named last changes fastest.
Arguments:
- output_grad: bfloat16 [2048, 4096], P(('groups', 'expert'), 'tower'), may hold values from -6 to 6
- gate_values: float32 [2048, 8], P(('groups', 'expert')), may hold values from 0.05 to 0.25
- expert_ids: int32 [2048, 8], P(('groups', 'expert')), may hold values from 0 to 15, all different within a row; in each aligned block of 128 rows (0 to 127, 128 to 255, ...) at most 112 rows name the same one
- pre_gate: bfloat16 [16, 16, 112, 768], P(('groups', 'expert')), may hold values from -6 to 6
- pre_up: bfloat16 [16, 16, 112, 768], P(('groups', 'expert')), may hold values from -6 to 6
- w_gate: bfloat16 [16, 4096, 768], P('expert', 'tower'), may hold values from -0.21875 to 0.21875
- w_up: bfloat16 [16, 4096, 768], P('expert', 'tower'), may hold values from -0.21875 to 0.21875
- w_down: bfloat16 [16, 768, 4096], P('expert', None, 'tower'), may hold values from -0.09375 to 0.09375
- visual: bfloat16 [256, 1152], P(('groups', 'expert')), may hold values from -0.5 to 0.5
- visual_rows: int32 [256], P(('groups', 'expert')), may hold values from 0 to 127
Outputs:
- input_grad: bfloat16 [2048, 4096], P(('groups', 'expert'), 'tower')
- projector_grad: float32 [1152, 4096], P(('groups', 'expert'), 'tower')
Inputs may be any that keep to these rules, and one draw needn't show every extreme that they name: `expert_ids`: each row names 8 different experts. Among the tokens of one block no expert is named by more than 112 rows, a bound that some block reaches. `visual_rows`: rows may repeat.
All inputs are finite; a program needn't handle non-finite values.
Results may differ from a plain program's by a relative error of at most 0.0033.
Values may be sent and summed in bfloat16 or wider, within the bound.
A program may use at most 128 MiB of HBM per device.

v0:
```python
import jax
import jax.numpy as jnp
from jax import lax
from jax.sharding import PartitionSpec as P


def hidden_grads(summed, gate_pre, up_pre):
    gate_float = gate_pre.astype(jnp.float32)
    up_float = up_pre.astype(jnp.float32)
    sigmoid_gate = jax.nn.sigmoid(gate_float)
    slope = sigmoid_gate * (1.0 + gate_float * (1.0 - sigmoid_gate))
    grad_gate = (summed * up_float * slope).astype(jnp.bfloat16)
    grad_up = (summed * gate_float * sigmoid_gate).astype(jnp.bfloat16)
    return (grad_gate, grad_up)


def per_device(
    output_grad,
    gate_values,
    expert_ids,
    pre_gate,
    pre_up,
    w_gate,
    w_up,
    w_down,
    visual,
    visual_rows,
):
    tok_rows, half_width = output_grad.shape
    top_count = expert_ids.shape[1]
    expert_count = lax.axis_size("expert")
    capacity = pre_gate.shape[2]
    hidden_units = pre_gate.shape[3]
    flat_ids = expert_ids.reshape(-1)
    onehot = (flat_ids[:, None] == jnp.arange(expert_count, dtype=jnp.int32)[None, :]).astype(
        jnp.int32
    )
    earlier = jnp.cumsum(onehot, axis=0) - onehot
    position = jnp.sum(earlier * onehot, axis=1)
    slot_index = flat_ids * capacity + position
    token_index = jnp.repeat(jnp.arange(tok_rows, dtype=jnp.int32), top_count)
    outgoing = (
        jnp.zeros((expert_count * capacity, half_width), jnp.bfloat16)
        .at[slot_index]
        .set(output_grad[token_index])
    )
    outgoing = outgoing.reshape(expert_count, capacity, half_width)
    incoming = lax.all_to_all(outgoing, "expert", split_axis=0, concat_axis=0, tiled=True)
    routed = incoming.reshape(-1, half_width)
    partial_value = jnp.einsum("rd,fd->rf", routed, w_down[0], preferred_element_type=jnp.float32)
    gate_pre = pre_gate[0].reshape(-1, hidden_units)
    up_pre = pre_up[0].reshape(-1, hidden_units)
    summed = lax.psum(partial_value, "tower")
    grad_gate, grad_up = hidden_grads(summed, gate_pre, up_pre)
    returning = jnp.einsum("rf,df->rd", grad_gate, w_gate[0], preferred_element_type=jnp.float32)
    returning = returning + jnp.einsum(
        "rf,df->rd", grad_up, w_up[0], preferred_element_type=jnp.float32
    )
    returning = returning.astype(jnp.bfloat16).reshape(expert_count, capacity, half_width)
    returned = lax.all_to_all(returning, "expert", split_axis=0, concat_axis=0, tiled=True)
    picked = returned.reshape(-1, half_width)[slot_index].reshape(tok_rows, top_count, half_width)
    combined = output_grad.astype(jnp.float32) + jnp.sum(
        gate_values[:, :, None] * picked.astype(jnp.float32), axis=1
    )
    input_grad = combined.astype(jnp.bfloat16)
    visual_grad = input_grad[visual_rows]
    features = lax.all_to_all(visual, "expert", split_axis=1, concat_axis=0, tiled=True)
    projector_grad = jnp.einsum(
        "rv,rd->vd",
        features,
        lax.all_gather(visual_grad, "expert", axis=0, tiled=True),
        preferred_element_type=jnp.float32,
    )
    return (input_grad, projector_grad)


def solution(mesh):
    in_specs = (
        P(("groups", "expert"), "tower"),
        P(("groups", "expert"), None),
        P(("groups", "expert"), None),
        P(("groups", "expert"), None, None, None),
        P(("groups", "expert"), None, None, None),
        P("expert", "tower", None),
        P("expert", "tower", None),
        P("expert", None, "tower"),
        P(("groups", "expert"), None),
        P(("groups", "expert")),
    )
    out_specs = (P(("groups", "expert"), "tower"), P(("groups", "expert"), "tower"))
    return jax.shard_map(
        per_device, mesh=mesh, in_specs=in_specs, out_specs=out_specs, check_vma=False
    )
```

profile of v0, /device:TPU:0, one launch (start us, length us, event | category | flops | bytes accessed | tf_op | source)
XLA Modules:
  0.0 536.7 jit_solution(10040518331896578876)
XLA Ops:
  7.2 0.0 copy-start
  7.2 0.0 all-reduce.2.cloned.1.call-start
  7.2 0.9 copy.17
  8.2 0.1 eq.29
  8.3 0.1 eq.25
  8.3 0.7 broadcast_multiply_fusion
  9.1 4.5 reduce-window.6
  13.6 0.1 slice.14
  13.6 0.1 copy.19
  13.8 0.1 copy.20
  13.9 0.1 broadcast_add_fusion
  14.0 0.1 copy.16
  14.1 0.1 mul.48
  14.2 0.1 reshape.105
  14.4 24.9 %scatter_custom_fusion = bf16[1792,2048]{1,0:T(8,128)(2,1)} fusion(s32[1024]{0:T(1024)S(1)} %bitcast.56, bf16[128,2048]{1,0:T(8,128)(2,1)} %param.10, s32[1024]{0:T(1024)S(1)} %broadcast_clamp_fusion.1, bf16[]{:T(256)} %constant.7.clone.1), kind=kCustom, calls=%fused_computation.20 | custom fusion | bytes 7340544 | tf_op jit(solution)/shard_map/scatter | solution.py:45
  39.2 0.0 copy-start.6
  39.2 169.8 %all_to_all.29 = bf16[16,112,2048]{2,1,0:T(8,128)(2,1)S(1)} all-to-all(bf16[16,112,2048]{2,1,0:T(8,128)(2,1)} %bitcast.49), channel_id=1, replica_groups=mesh['groups'=1,'expert'=16,'tower'=2] {'expert'}, dimensions={0} | all-to-all | bytes 14680064 | tf_op jit(solution)/shard_map/all_to_all | solution.py:48
  209.0 0.0 copy-done.6
  209.0 7.7 %fusion.16 = f32[1792,768]{1,0:T(8,128)} fusion(bf16[1792,2048]{1,0:T(8,128)(2,1)S(1)} %bitcast.51, bf16[1,768,2048]{2,1,0:T(8,128)(2,1)S(1)} %copy-done.6), kind=kOutput, calls=%fused_computation.26 | convolution fusion | flops 5637144576 | bytes 15990784 | tf_op jit(solution)/shard_map/rd,fd->rf/dot_general | solution.py:50
  216.7 0.0 all-reduce.2.cloned.1.call-update
  216.7 29.0 %all-reduce.2.cloned.1.call-done = f32[1792,768]{1,0:T(8,128)} async-done(((f32[1792,768]{1,0:T(8,128)}), f32[1792,768]{1,0:T(8,128)}) %all-reduce.2.cloned.1.call-update) | async-done | bytes 5505040 | tf_op jit(solution)/shard_map/psum | solution.py:53
  245.7 0.0 copy-done
  245.7 0.0 copy-start.5
  245.7 15.6 %fusion.14 = f32[1792,2048]{1,0:T(8,128)} fusion(bf16[1,2048,768]{2,1,0:T(8,128)(2,1)S(1)} %copy-done, bf16[1792,768]{1,0:T(8,128)(2,1)} %bitcast.60, f32[1792,768]{1,0:T(8,128)} %all-reduce.2.cloned.1.call-done, bf16[1792,768]{1,0:T(8,128)(2,1)} %bitcast.59), kind=kOutput, calls=%fused_computation.24 | convolution fusion | flops 5653659648 | bytes 28835840 | tf_op jit(solution)/shard_map/rf,df->rd/dot_general | solution.py:55
  261.4 0.0 copy-done.5
  261.4 13.3 %add_convert_fusion = bf16[1792,2048]{1,0:T(8,128)(2,1)} fusion(f32[1792,2048]{1,0:T(8,128)} %fusion.14, bf16[1,2048,768]{2,1,0:T(8,128)(2,1)} %param.16, f32[1792,768]{1,0:T(8,128)S(1)} %copy-done.5, bf16[1792,768]{1,0:T(8,128)(2,1)} %bitcast.61), kind=kOutput, calls=%fused_computation.4 | convolution fusion | flops 5654118400 | bytes 33423360 | tf_op jit(solution)/shard_map/rf,df->rd/dot_general | solution.py:56
  274.7 0.0 copy-start.4
  274.7 0.0 copy-start.7
  274.7 7.0 %all-to-all-start.1 = ((bf16[16,112,2048]{2,1,0:T(8,128)(2,1)}), bf16[16,112,2048]{2,1,0:T(8,128)(2,1)}, u32[]{:S(2)}, u32[]{:S(2)}) async-start(bf16[16,112,2048]{2,1,0:T(8,128)(2,1)} %bitcast.50), calls=%async_computation.1 | async-start | bytes 14680064 | tf_op jit(solution)/shard_map/all_to_all | solution.py:60
  281.7 0.3 all-gather.3.cloned.1.call-start
  281.9 0.0 copy-done.4
  282.0 0.1 copy.15
  282.1 0.0 copy-done.7
  282.1 139.2 %all-to-all-done.1 = bf16[16,112,2048]{2,1,0:T(8,128)(2,1)} async-done(((bf16[16,112,2048]{2,1,0:T(8,128)(2,1)}), bf16[16,112,2048]{2,1,0:T(8,128)(2,1)}, u32[]{:S(2)}, u32[]{:S(2)}) %all-to-all-start.1) | async-done | bytes 7340064 | tf_op jit(solution)/shard_map/all_to_all | solution.py:60
  421.3 0.0 copy-start.1
  421.3 13.0 %gather_fusion = bf16[1024,2048]{1,0:T(8,128)(2,1)} fusion(bf16[1792,2048]{1,0:T(8,128)(2,1)} %bitcast.14, s32[1024]{0:T(1024)S(1)} %broadcast_clamp_fusion), kind=kCustom, calls=%fused_computation.1 | custom fusion | bytes 8392704 | tf_op jit(solution)/shard_map/gather | solution.py:61
  434.3 0.0 copy-start.2
  434.3 0.0 copy-start.3
  434.3 6.6 %fusion = f32[128,2048]{1,0:T(8,128)S(1)} fusion(bf16[1024,2048]{1,0:T(8,128)(2,1)} %gather_fusion, f32[128,8]{1,0:T(8,128)S(1)} %copy.15), kind=kLoop, calls=%fused_computation.6 | loop fusion | flops 6029312 | bytes 5246976 | tf_op jit(solution)/shard_map/reduce_sum | solution.py:62
  440.9 0.0 copy-done.2
  440.9 0.9 add_convert_fusion.1
  441.8 2.4 gather_fusion.1
  444.2 0.0 all-gather.3.cloned.1.call-update
  444.2 0.0 copy-done.3
  444.2 0.1 all_to_all.22
  444.4 40.8 %all_to_all.30 = bf16[16,16,72]{2,0,1:T(8,128)(2,1)S(1)} all-to-all(bf16[16,16,72]{2,0,1:T(8,128)(2,1)S(1)} %copy.21), channel_id=1, replica_groups=mesh['groups'=1,'expert'=16,'tower'=2] {'expert'}, dimensions={1} | all-to-all | bytes 73728 | tf_op jit(solution)/shard_map/all_to_all | solution.py:67
  485.2 42.3 %all-gather.3.cloned.1.call-done = bf16[256,2048]{1,0:T(8,128)(2,1)} async-done(((bf16[16,2048]{1,0:T(8,128)(2,1)}), bf16[256,2048]{1,0:T(8,128)(2,1)}) %all-gather.3.cloned.1.call-update) | async-done | bytes 1048592 | tf_op jit(solution)/shard_map/all_gather | solution.py:71
  527.5 2.4 convolution_bitcast_fusion
  529.8 0.0 copy-done.1
  (12 shorter events, 0.1 us)
Async XLA Ops:
  7.2 238.6 %copy-start = (bf16[1,2048,768]{2,1,0:T(8,128)(2,1)S(1)}, bf16[1,2048,768]{2,1,0:T(8,128)(2,1)}, u32[]{:S(2)}) copy-start(bf16[1,2048,768]{2,1,0:T(8,128)(2,1)} %param.15) | copy-start | bytes 9437188
  7.2 238.6 %all-reduce.2.cloned.1.call-start = ((), (), s32[]{:S(2)}) async-start(), calls=%async_computation.3 | async-start | bytes 11010048 | tf_op jit(solution)/shard_map/psum | solution.py:53
  39.2 169.8 %copy-start.6 = (bf16[1,768,2048]{2,1,0:T(8,128)(2,1)S(1)}, bf16[1,768,2048]{2,1,0:T(8,128)(2,1)}, u32[]{:S(2)}) copy-start(bf16[1,768,2048]{2,1,0:T(8,128)(2,1)} %param.17) | copy-start | bytes 9437188
  245.7 15.6 %copy-start.5 = (f32[1792,768]{1,0:T(8,128)S(1)}, f32[1792,768]{1,0:T(8,128)}, u32[]{:S(2)}) copy-start(f32[1792,768]{1,0:T(8,128)} %all-reduce.2.cloned.1.call-done) | copy-start | bytes 16515076
  274.7 7.2 %copy-start.4 = (f32[128,8]{0,1:T(8,128)S(1)}, f32[128,8]{0,1:T(8,128)}, u32[]{:S(2)}) copy-start(f32[128,8]{0,1:T(8,128)} %param.11) | copy-start | bytes 12292
  274.7 7.3 %copy-start.7 = (s32[16]{0:T(128)S(1)}, s32[16]{0:T(128)}, u32[]{:S(2)}) copy-start(s32[16]{0:T(128)} %param.19) | copy-start | bytes 196
  274.7 146.6 %all-to-all-start.1 = ((bf16[16,112,2048]{2,1,0:T(8,128)(2,1)}), bf16[16,112,2048]{2,1,0:T(8,128)(2,1)}, u32[]{:S(2)}, u32[]{:S(2)}) async-start(bf16[16,112,2048]{2,1,0:T(8,128)(2,1)} %bitcast.50), calls=%async_computation.1 | async-start | bytes 14680064 | tf_op jit(solution)/shard_map/all_to_all | solution.py:60
  281.7 245.8 %all-gather.3.cloned.1.call-start = ((), (), s32[]{:S(2)}) async-start(), calls=%async_computation.4 | async-start | bytes 1114112 | tf_op jit(solution)/shard_map/all_gather | solution.py:71
  421.3 108.5 %copy-start.1 = (bf16[1,2048,768]{2,1,0:T(8,128)(2,1)S(1)}, bf16[1,2048,768]{2,1,0:T(8,128)(2,1)}, u32[]{:S(2)}) copy-start(bf16[1,2048,768]{2,1,0:T(8,128)(2,1)} %param.15) | copy-start | bytes 9437188
  434.3 6.6 %copy-start.2 = (bf16[128,2048]{1,0:T(8,128)(2,1)S(1)}, bf16[128,2048]{1,0:T(8,128)(2,1)}, u32[]{:S(2)}) copy-start(bf16[128,2048]{1,0:T(8,128)(2,1)} %param.10) | copy-start | bytes 1572868
  434.3 9.9 %copy-start.3 = (bf16[16,1152]{1,0:T(8,128)(2,1)S(1)}, bf16[16,1152]{1,0:T(8,128)(2,1)}, u32[]{:S(2)}) copy-start(bf16[16,1152]{1,0:T(8,128)(2,1)} %param.18) | copy-start | bytes 110596
Sparse Core Ops, SparseCore 0:
  216.8 28.8 all-reduce.1
  444.3 83.0 all-gather.2
where the time goes:
time: 537 us
  blocking collectives  211 us (39%)
  waiting for transfers between devices  211 us (39%)
  local copies, waits for them, and re-layouts  42.3 us (8%)
  matrix products  39 us (7%)
  between operations  14.2 us (3%)
  other arithmetic  12.9 us (2%)
  starting transfers between devices  7.26 us (1%)
    all_to_all x1, blocking collectives, per_device(): lax.all_to_all(outgoing, 'expert', split_axis=0, concat_axis=0, tiled=True)  170 us
    all_to_all x1, waiting for transfers between devices, per_device(): lax.all_to_all(returning, 'expert', split_axis=0, concat_axis=0, tiled=True)  139 us
    all_gather x1, waiting for transfers between devices, per_device(): lax.all_gather(visual_grad, 'expert', axis=0, tiled=True)  42.3 us
    all_to_all x1, blocking collectives, per_device(): lax.all_to_all(visual, 'expert', split_axis=1, concat_axis=0, tiled=True)  40.8 us
    psum x1, waiting for transfers between devices, per_device(): summed = lax.psum(partial_value, 'tower')  29 us
    scatter x1, local copies, waits for them, and re-layouts, per_device(): outgoing = jnp.zeros((expert_count * capacity, half_width), jnp.bfloat16)...  24.9 us
    dot_general x1, matrix products, per_device(): jnp.einsum('rf,df->rd', grad_gate, w_gate[0], preferred_element_type=jnp....  15.6 us
    dot_general x1, matrix products, per_device(): jnp.einsum('rf,df->rd', grad_up, w_up[0], preferred_element_type=jnp.floa...  13.3 us
  transfers between devices with their start and end apart: 3, of which 3 were waited for; matrix products, arithmetic and copies ran while one was open for 0% of the time, Pallas kernels for 0%

commit v1 on v0

--- a/solution.py
+++ b/solution.py
@@ -74,7 +74,62 @@
     return (input_grad, projector_grad)
 
 
+def per_device_tokens(
+    output_grad,
+    gate_values,
+    expert_ids,
+    pre_gate,
+    pre_up,
+    w_gate,
+    w_up,
+    w_down,
+    visual,
+    visual_rows,
+):
+    tok_rows, half_width = output_grad.shape
+    blocks = lax.axis_size("expert")
+    capacity, hidden_units = pre_gate.shape[2:]
+    me = lax.axis_index("expert")
+    every_grad = lax.all_gather(output_grad, "expert", axis=0, tiled=True)
+    every_id = lax.all_gather(expert_ids, "expert", axis=0, tiled=True)
+    every_value = lax.all_gather(gate_values, "expert", axis=0, tiled=True)
+    named = every_id == me
+    weight = jnp.sum(jnp.where(named, every_value, 0.0), axis=1)
+    here = jnp.any(named, axis=1).reshape(blocks, tok_rows)
+    count = here.astype(jnp.int32)
+    position = jnp.cumsum(count, axis=1) - count
+    position = jnp.where(here, position, -1)
+    onehot = (position[:, :, None] == jnp.arange(capacity, dtype=jnp.int32)).astype(jnp.bfloat16)
+    gate_pre = jnp.einsum("btc,bcf->btf", onehot, pre_gate[0]).reshape(-1, hidden_units)
+    up_pre = jnp.einsum("btc,bcf->btf", onehot, pre_up[0]).reshape(-1, hidden_units)
+    partial_value = jnp.einsum(
+        "rd,fd->rf", every_grad, w_down[0], preferred_element_type=jnp.float32
+    )
+    summed = lax.psum(partial_value, "tower")
+    grad_gate, grad_up = hidden_grads(summed, gate_pre, up_pre)
+    returning = jnp.einsum("rf,df->rd", grad_gate, w_gate[0], preferred_element_type=jnp.float32)
+    returning = returning + jnp.einsum(
+        "rf,df->rd", grad_up, w_up[0], preferred_element_type=jnp.float32
+    )
+    returning = (returning * weight[:, None]).astype(jnp.bfloat16)
+    total = lax.psum_scatter(returning, "expert", scatter_dimension=0, tiled=True)
+    input_grad = (output_grad.astype(jnp.float32) + total.astype(jnp.float32)).astype(jnp.bfloat16)
+    return (input_grad, projector(input_grad, visual, visual_rows))
+
+
+def projector(input_grad, visual, visual_rows):
+    visual_grad = input_grad[visual_rows]
+    features = lax.all_to_all(visual, "expert", split_axis=1, concat_axis=0, tiled=True)
+    return jnp.einsum(
+        "rv,rd->vd",
+        features,
+        lax.all_gather(visual_grad, "expert", axis=0, tiled=True),
+        preferred_element_type=jnp.float32,
+    )
+
+
 def solution(mesh):
+    per_rank = per_device_tokens if mesh.shape["expert"] <= 16 else per_device
     in_specs = (
         P(("groups", "expert"), "tower"),
         P(("groups", "expert"), None),
@@ -89,5 +144,5 @@
     )
     out_specs = (P(("groups", "expert"), "tower"), P(("groups", "expert"), "tower"))
     return jax.shard_map(
-        per_device, mesh=mesh, in_specs=in_specs, out_specs=out_specs, check_vma=False
+        per_rank, mesh=mesh, in_specs=in_specs, out_specs=out_specs, check_vma=False
     )

time: 537 us -> 501 us (0.933)
  waiting for transfers between devices: 211 us -> 337 us
  blocking collectives: 211 us -> 89.5 us
  local copies, waits for them, and re-layouts: 42.3 us -> 3.76 us
  matrix products: 39 us -> 54.2 us
  other arithmetic: 12.9 us -> 2.49 us
  starting transfers between devices: 7.26 us -> 0.16 us
    all_to_all x2 -> x1, blocking collectives: 211 us -> 15.3 us  [projector(): lax.all_to_all(visual, 'expert', split_axis=1, concat_axis=0, tiled=True)]
    reduce_scatter x0 -> x1, waiting for transfers between devices: none -> 175 us  [per_device_tokens(): lax.psum_scatter(returning, 'expert', scatter_dimension=0, tiled=True)]
    all_to_all x1 -> x0, waiting for transfers between devices: 139 us -> none  [per_device(): lax.all_to_all(returning, 'expert', split_axis=0, concat_axis=0, tiled=True)]
    all_gather x1 -> x2, waiting for transfers between devices: 42.3 us -> 161 us  [the longest x1 118 us: per_device_tokens(): every_grad = lax.all_gather(output_grad, 'expert', axis=0, tiled=True)]
    all_gather x0 -> x2, blocking collectives: none -> 74.1 us  [the longest x1 38.1 us: per_device_tokens(): every_id = lax.all_gather(expert_ids, 'expert', axis=0, tiled=True)]
    psum x1, waiting for transfers between devices: 29 us -> 0.01 us  [per_device_tokens(): summed = lax.psum(partial_value, 'tower')]
    scatter x1 -> x0, local copies, waits for them, and re-layouts: 24.9 us -> none  [per_device(): outgoing = jnp.zeros((expert_count * capacity, half_width), jnp.bfloat16)...]
    dot_general x4 -> x6, matrix products: 39 us -> 54.2 us  [the longest x1 17.4 us: per_device_tokens(): jnp.einsum('rf,df->rd', grad_gate, w_gate[0], preferred_element_type=jnp....]
  transfers between devices with their start and end apart: 3 -> 4, of which waited for: 3 -> 3; matrix products, arithmetic and copies ran while one was open for 0% -> 2% of each run, Pallas kernels for 0% -> 0%
where the time goes in v1:
time: 501 us; the launch traced here: 500 us
  waiting for transfers between devices  337 us (67%)
  blocking collectives  89.5 us (18%)
  matrix products  54.2 us (11%)
  between operations  13.8 us (3%)
    reduce_scatter x1, waiting for transfers between devices, per_device_tokens(): lax.psum_scatter(returning, 'expert', scatter_dimension=0, tiled=True)  175 us
    all_gather x1, waiting for transfers between devices, per_device_tokens(): every_grad = lax.all_gather(output_grad, 'expert', axis=0, tiled=True)  118 us
    all_gather x1, waiting for transfers between devices, projector(): lax.all_gather(visual_grad, 'expert', axis=0, tiled=True)  42.3 us
    all_gather x1, blocking collectives, per_device_tokens(): every_id = lax.all_gather(expert_ids, 'expert', axis=0, tiled=True)  38.1 us
    all_gather x1, blocking collectives, per_device_tokens(): every_value = lax.all_gather(gate_values, 'expert', axis=0, tiled=True)  36 us
    dot_general x1, matrix products, per_device_tokens(): jnp.einsum('rf,df->rd', grad_gate, w_gate[0], preferred_element_type=jnp....  17.4 us
    dot_general x1, matrix products, per_device_tokens(): jnp.einsum('rf,df->rd', grad_up, w_up[0], preferred_element_type=jnp.floa...  15.4 us
    all_to_all x1, blocking collectives, projector(): lax.all_to_all(visual, 'expert', split_axis=1, concat_axis=0, tiled=True)  15.3 us
  transfers between devices with their start and end apart: 4, of which 3 were waited for; matrix products, arithmetic and copies ran while one was open for 2% of the time, Pallas kernels for 0%

profile of v1, /device:TPU:0, one launch (start us, length us, event | category | flops | bytes accessed | tf_op | source)
XLA Modules:
  0.0 500.4 jit_solution(11331397819199029121)
XLA Ops:
  7.2 0.0 copy-start
  7.2 0.0 all-gather.4.cloned.1.call-start
  7.2 0.7 all-gather.4.cloned.1.call-update
  7.9 0.0 all-reduce.2.cloned.1.call-start
  8.0 118.4 %all-gather.4.cloned.1.call-done = bf16[2048,2048]{1,0:T(8,128)(2,1)} async-done(((bf16[128,2048]{1,0:T(8,128)(2,1)}), bf16[2048,2048]{1,0:T(8,128)(2,1)}) %all-gather.4.cloned.1.call-update) | async-done | bytes 8388624 | tf_op jit(solution)/shard_map/all_gather | solution.py:93
  126.3 11.8 %fusion.14 = f32[2048,768]{1,0:T(8,128)} fusion(bf16[2048,2048]{1,0:T(8,128)(2,1)} %all-gather.4.cloned.1.call-done, bf16[1,768,2048]{2,1,0:T(8,128)(2,1)} %param.17), kind=kOutput, calls=%fused_computation.18 | convolution fusion | flops 6442450944 | bytes 17825792 | tf_op jit(solution)/shard_map/rd,fd->rf/dot_general | solution.py:105
  138.2 0.0 copy-start.4
  138.2 0.0 copy-start.5
  138.2 0.0 all-reduce.2.cloned.1.call-update
  138.2 0.0 reduce-scatter.2.cloned.1.call-start
  138.2 0.6 copy-done.4
  138.8 38.1 %all_gather.13 = s32[2048,8]{0,1:T(8,128)S(1)} all-gather(s32[128,8]{0,1:T(8,128)S(1)} %copy-done.4), channel_id=1, replica_groups=mesh['groups'=1,'expert'=16,'tower'=2] {'expert'}, dimensions={0}, use_global_device_ids=true | all-gather | bytes 69632 | tf_op jit(solution)/shard_map/all_gather | solution.py:94
  177.0 0.0 copy-done.5
  177.0 36.0 %all_gather.14 = f32[2048,8]{0,1:T(8,128)S(1)} all-gather(f32[128,8]{0,1:T(8,128)S(1)} %copy-done.5), channel_id=1, replica_groups=mesh['groups'=1,'expert'=16,'tower'=2] {'expert'}, dimensions={0}, use_global_device_ids=true | all-gather | bytes 69632 | tf_op jit(solution)/shard_map/all_gather | solution.py:95
  213.0 0.3 reduce_window_sum.11
  213.3 0.0 copy-start.2
  213.3 4.6 fusion.18
  217.9 0.0 copy-done.2
  217.9 2.7 fusion.20
  220.6 0.0 all-reduce.2.cloned.1.call-done
  220.6 0.0 copy-done
  220.6 17.4 %fusion.10 = f32[2048,2048]{1,0:T(8,128)} fusion(bf16[2048,768]{1,0:T(8,128)(2,1)} %bitcast.32, f32[2048,768]{1,0:T(8,128)} %all-reduce.2.cloned.1.call-done, bf16[2048,768]{1,0:T(8,128)(2,1)} %bitcast.34, bf16[1,2048,768]{2,1,0:T(8,128)(2,1)S(1)} %copy-done), kind=kOutput, calls=%fused_computation.15 | convolution fusion | flops 6461325312 | bytes 32505856 | tf_op jit(solution)/shard_map/rf,df->rd/dot_general | solution.py:110
  238.0 15.4 %multiply_convert_fusion = bf16[2048,2048]{1,0:T(8,128)(2,1)} fusion(f32[2048,2048]{1,0:T(8,128)} %fusion.10, f32[2048]{0:T(1024)S(1)} %get-tuple-element.2, f32[2048,768]{1,0:T(8,128)} %all-reduce.2.cloned.1.call-done, bf16[2048,768]{1,0:T(8,128)(2,1)} %bitcast.33, bf16[1,2048,768]{2,1,0:T(8,128)(2,1)} %param.16), kind=kOutput, calls=%fused_computation.1 | convolution fusion | flops 6466043904 | bytes 37756928 | tf_op jit(solution)/shard_map/rf,df->rd/dot_general | solution.py:111
  253.3 0.0 copy-start.6
  253.3 0.0 copy-start.3
  253.3 0.0 copy-start.1
  253.4 0.0 reduce-scatter.2.cloned.1.call-update
  253.4 0.0 all-gather.6.cloned.1.call-start
  253.4 0.6 copy-done.6
  254.0 175.1 %reduce-scatter.2.cloned.1.call-done = bf16[128,2048]{1,0:T(8,128)(2,1)} async-done(((bf16[2048,2048]{1,0:T(8,128)(2,1)}), bf16[128,2048]{1,0:T(8,128)(2,1)}) %reduce-scatter.2.cloned.1.call-update) | async-done | bytes 524304 | tf_op jit(solution)/shard_map/reduce_scatter | solution.py:115
  429.1 2.1 add_convert_fusion
  431.3 2.4 gather_fusion
  433.7 0.0 all-gather.6.cloned.1.call-update
  433.7 0.0 copy-done.3
  433.7 0.1 all_to_all.14
  433.9 15.3 %all_to_all.19 = bf16[16,16,72]{2,0,1:T(8,128)(2,1)S(1)} all-to-all(bf16[16,16,72]{2,0,1:T(8,128)(2,1)S(1)} %copy.12), channel_id=1, replica_groups=mesh['groups'=1,'expert'=16,'tower'=2] {'expert'}, dimensions={1} | all-to-all | bytes 73728 | tf_op jit(solution)/shard_map/all_to_all | solution.py:122
  449.2 42.3 %all-gather.6.cloned.1.call-done = bf16[256,2048]{1,0:T(8,128)(2,1)} async-done(((bf16[16,2048]{1,0:T(8,128)(2,1)}), bf16[256,2048]{1,0:T(8,128)(2,1)}) %all-gather.6.cloned.1.call-update) | async-done | bytes 1048592 | tf_op jit(solution)/shard_map/all_gather | solution.py:126
  491.5 2.4 convolution_bitcast_fusion
  493.9 0.0 copy-done.1
  (7 shorter events, 0.1 us)
Async XLA Ops:
  7.2 213.4 %copy-start = (bf16[1,2048,768]{2,1,0:T(8,128)(2,1)S(1)}, bf16[1,2048,768]{2,1,0:T(8,128)(2,1)}, u32[]{:S(2)}) copy-start(bf16[1,2048,768]{2,1,0:T(8,128)(2,1)} %param.15) | copy-start | bytes 9437188
  7.2 119.2 %all-gather.4.cloned.1.call-start = ((), (), s32[]{:S(2)}) async-start(), calls=%async_computation.2 | async-start | bytes 8912896 | tf_op jit(solution)/shard_map/all_gather | solution.py:93
  7.9 212.7 %all-reduce.2.cloned.1.call-start = ((), (), s32[]{:S(2)}) async-start(), calls=%async_computation.3 | async-start | bytes 12582912 | tf_op jit(solution)/shard_map/psum | solution.py:108
  138.2 0.7 copy-start.4
  138.2 38.8 %copy-start.5 = (f32[128,8]{0,1:T(8,128)S(1)}, f32[128,8]{0,1:T(8,128)}, u32[]{:S(2)}) copy-start(f32[128,8]{0,1:T(8,128)} %param.11) | copy-start | bytes 12292
  138.2 291.0 %reduce-scatter.2.cloned.1.call-start = ((), (), s32[]{:S(2)}) async-start(), calls=%async_computation.4 | async-start | bytes 8912896 | tf_op jit(solution)/shard_map/reduce_scatter | solution.py:115
  213.3 4.6 copy-start.2
  253.3 0.7 copy-start.6
  253.3 180.3 %copy-start.3 = (bf16[16,1152]{1,0:T(8,128)(2,1)S(1)}, bf16[16,1152]{1,0:T(8,128)(2,1)}, u32[]{:S(2)}) copy-start(bf16[16,1152]{1,0:T(8,128)(2,1)} %param.18) | copy-start | bytes 110596
  253.3 240.5 %copy-start.1 = (bf16[1,2048,768]{2,1,0:T(8,128)(2,1)S(1)}, bf16[1,2048,768]{2,1,0:T(8,128)(2,1)}, u32[]{:S(2)}) copy-start(bf16[1,2048,768]{2,1,0:T(8,128)(2,1)} %param.15) | copy-start | bytes 9437188
  253.4 238.1 %all-gather.6.cloned.1.call-start = ((), (), s32[]{:S(2)}) async-start(), calls=%async_computation.5 | async-start | bytes 1114112 | tf_op jit(solution)/shard_map/all_gather | solution.py:126
Sparse Core Ops, SparseCore 0:
  10.8 115.5 all-gather.3
  138.3 30.2 all-reduce.1
  253.5 175.5 reduce-scatter.1
  433.8 57.6 all-gather.5

commit v2 on v0

--- a/solution.py
+++ b/solution.py
@@ -1,6 +1,8 @@
 import jax
 import jax.numpy as jnp
 from jax import lax
+from jax.experimental import pallas as pl
+from jax.experimental.pallas import tpu as pltpu
 from jax.sharding import PartitionSpec as P
 
 
@@ -74,7 +76,322 @@
     return (input_grad, projector_grad)
 
 
+def expert_kernel(
+    og, info, pg, pu, wg, wu, wd, out,
+    held, contrib, gate_tok, up_tok, own_sum, half_out, half_in, grad_g, grad_u, l1, l2, l3,
+    zs, zr, xs, xr, ys, yr, fs, fr, hs, hr, s1, r1, s2, r2, s3, r3,
+):
+    zl, tok, half = held.shape[2:]
+    hid = wd.shape[0]
+    cap = pg.shape[2]
+    rows = zl * tok
+    group, me, core = lax.axis_index("groups"), lax.axis_index("expert"), lax.axis_index("tower")
+    z, y, x = lax.div(me, 4), lax.rem(lax.div(me, 2), 2), lax.rem(me, 2)
+    q, qx = y * 2 + x, y * 2 + 1 - x
+    qy, qd = (1 - y) * 2 + x, (1 - y) * 2 + 1 - x
+
+    def dev(e):
+        return (group, e, core)
+
+    xn, yn = dev(z * 4 + qx), dev(z * 4 + qy)
+    other = (group, me, 1 - core)
+    zto = [lax.rem(z + k, 4) for k in range(4)]
+    zfrom = [lax.rem(z + 4 - k, 4) for k in range(4)]
+    zdev = [dev(zto[k] * 4 + q) for k in range(4)]
+
+    def remote(src, dst, ss, rs, device):
+        return pltpu.make_async_remote_copy(
+            src_ref=src, dst_ref=dst, send_sem=ss, recv_sem=rs,
+            device_id=device, device_id_type=pl.DeviceIdType.MESH,
+        )
+
+    barrier = pltpu.get_barrier_semaphore()
+    for device in (xn, yn, other, zdev[1], zdev[2], zdev[3]):
+        pl.semaphore_signal(barrier, inc=1, device_id=device, device_id_type=pl.DeviceIdType.MESH)
+    for h in range(2):
+        held[h, q, z] = og[:, h * half : (h + 1) * half]
+    pl.semaphore_wait(barrier, 6)
+
+    started = []
+
+    def go(copy):
+        copy.start()
+        started.append(copy)
+        return copy
+
+    def to_x(k, h):
+        block = held.at[h, q, zfrom[k]]
+        return go(remote(block, block, xs.at[k, h], xr.at[k, h], xn))
+
+    def to_y(k, h):
+        block = held.at[h, q, zfrom[k]]
+        return go(remote(block, block, ys.at[k, h], yr.at[k, h], yn))
+
+    zc, xc, yc, fc = {}, {}, {}, {}
+
+    def forward(k):
+        xc[k, 0].wait_recv()
+        block = held.at[0, qx, zfrom[k]]
+        fc[k, 0] = go(remote(block, block, fs.at[k, 0], fr.at[k, 0], yn))
+        yc[k, 1].wait_recv()
+        block = held.at[1, qy, zfrom[k]]
+        fc[k, 1] = go(remote(block, block, fs.at[k, 1], fr.at[k, 1], xn))
+
+    for k in (1, 3, 2):
+        for h in range(2):
+            block = held.at[h, q, z]
+            zc[k, h] = remote(block, block, zs.at[k, h], zr.at[k, h], zdev[k])
+    xc[0, 0], yc[0, 1] = to_x(0, 0), to_y(0, 1)
+    for k in (1, 3, 2):
+        go(zc[k, 0])
+        go(zc[k, 1])
+    xc[0, 1], yc[0, 0] = to_x(0, 1), to_y(0, 0)
+
+    @pl.loop(0, 4)
+    def _(zi):
+        @pl.loop(0, 4)
+        def _(qi):
+            place = info[zi * 4 + qi, :, 1:2]
+            slot = lax.broadcasted_iota(jnp.int32, (tok, cap), 1).astype(jnp.float32)
+            spread = jnp.where(place == slot, 1.0, 0.0).astype(jnp.bfloat16)
+            for pre, dest in ((pg, gate_tok), (pu, up_tok)):
+                dest[qi, zi] = jnp.dot(
+                    spread, pre[zi, qi], preferred_element_type=jnp.float32
+                ).astype(jnp.bfloat16)
+
+    done = None
+    for k in (1, 3, 2):
+        zc[k, 0].wait_recv()
+        xc[k, 0] = to_x(k, 0)
+        zc[k, 1].wait_recv()
+        yc[k, 1] = to_y(k, 1)
+        xc[k, 1], yc[k, 0] = to_x(k, 1), to_y(k, 0)
+        forward(0 if done is None else done)
+        done = k
+
+    hc = []
+
+    def hidden(g, qq):
+        @pl.loop(0, hid // 256)
+        def _(n):
+            cols = pl.ds(pl.multiple_of(n * 256, 256), 256)
+            total = jnp.zeros((rows, 256), jnp.float32)
+            for h in range(2):
+                total = total + lax.dot_general(
+                    held[h, qq].reshape(rows, half),
+                    wd[cols, h * half : (h + 1) * half],
+                    (((1,), (1,)), ((), ())),
+                    preferred_element_type=jnp.float32,
+                )
+            own_sum[g % 2, :, cols] = total
+            half_out[g, :, cols] = total.astype(jnp.bfloat16)
+
+        hc.append(go(remote(half_out.at[g], half_in.at[g], hs.at[g], hr.at[g], other)))
+
+    def finish(g, qq):
+        hc[g].wait_recv()
+
+        @pl.loop(0, zl)
+        def _(zi):
+            part = pl.ds(pl.multiple_of(zi * tok, tok), tok)
+            summed = own_sum[g % 2, part, :] + half_in[g, part, :].astype(jnp.float32)
+            summed = summed * info[zi * 4 + qq, :, 0:1]
+            gate = gate_tok[qq, zi].astype(jnp.float32)
+            up = up_tok[qq, zi].astype(jnp.float32)
+            sig = jax.nn.sigmoid(gate)
+            grad_g[part, :] = (summed * up * (sig * (1.0 + gate * (1.0 - sig)))).astype(jnp.bfloat16)
+            grad_u[part, :] = (summed * gate * sig).astype(jnp.bfloat16)
+
+        for h in range(2):
+
+            @pl.loop(0, half // 256)
+            def _(n):
+                wrows = pl.ds(pl.multiple_of(h * half + n * 256, 256), 256)
+                cols = pl.ds(pl.multiple_of(n * 256, 256), 256)
+                total = jnp.zeros((rows, 256), jnp.float32)
+                for grad, weight in ((grad_g, wg), (grad_u, wu)):
+                    total = total + lax.dot_general(
+                        grad[...], weight[wrows, :],
+                        (((1,), (1,)), ((), ())),
+                        preferred_element_type=jnp.float32,
+                    )
+                contrib[h, qq, :, :, cols] = total.reshape(zl, tok, 256).astype(jnp.bfloat16)
+
+    order = (2, 1, 3, 0)
+    c1, c2, c3 = {}, {}, {}
+
+    def first(h, g, qq, device):
+        for k in order:
+            c1[h, g, k] = go(
+                remote(
+                    contrib.at[h, qq, zto[k]], l1.at[h, g, k],
+                    s1.at[h * 2 + g, k], r1.at[h * 2 + g, k], device,
+                )
+            )
+
+    hidden(0, q)
+    forward(2)
+    for k in range(4):
+        xc[k, 1].wait_recv()
+    hidden(1, qx)
+    finish(0, q)
+    for k in range(4):
+        yc[k, 0].wait_recv()
+    hidden(2, qy)
+    finish(1, qx)
+    first(1, 0, qx, xn)
+    for k in range(4):
+        fc[k, 0].wait_recv()
+        fc[k, 1].wait_recv()
+    hidden(3, qd)
+    finish(2, qy)
+    first(0, 0, qy, yn)
+    finish(3, qd)
+    first(0, 1, qd, yn)
+    first(1, 1, qd, xn)
+
+    step = 32
+
+    def add(dest, parts):
+        @pl.loop(0, tok // step)
+        def _(i):
+            part = pl.ds(pl.multiple_of(i * step, step), step)
+            dest(part, sum(p(part).astype(jnp.float32) for p in parts))
+
+    def combine(h, qq, zi, parts):
+        def store(part, value):
+            contrib[h, qq, zi, part, :] = value.astype(jnp.bfloat16)
+
+        add(store, [lambda part: contrib[h, qq, zi, part, :]] + parts)
+
+    def second(k):
+        for h, qq, device in ((0, qx, xn), (1, qy, yn)):
+            c1[h, 1, k].wait_recv()
+            combine(h, qq, zto[k], [lambda part: l1[h, 1, k, part, :]])
+            c2[h, k] = go(
+                remote(contrib.at[h, qq, zto[k]], l2.at[h, k], s2.at[h, k], r2.at[h, k], device)
+            )
+
+    def third(k):
+        for h in range(2):
+            c1[h, 0, k].wait_recv()
+            c2[h, k].wait_recv()
+            if k:
+                combine(
+                    h, q, zto[k],
+                    [lambda part: l1[h, 0, k, part, :], lambda part: l2[h, k, part, :]],
+                )
+                c3[h, k] = go(
+                    remote(contrib.at[h, q, zto[k]], l3.at[h, k], s3.at[h, k], r3.at[h, k], zdev[k])
+                )
+
+    second(order[0])
+    second(order[1])
+    third(order[0])
+    second(order[2])
+    third(order[1])
+    second(order[3])
+    third(order[2])
+    third(order[3])
+    for h in range(2):
+        for k in (1, 2, 3):
+            c3[h, k].wait_recv()
+
+        def store(part, value):
+            out[part, h * half : (h + 1) * half] = value.astype(jnp.bfloat16)
+
+        add(
+            store,
+            [
+                lambda part: contrib[h, q, z, part, :],
+                lambda part: l1[h, 0, 0, part, :],
+                lambda part: l2[h, 0, part, :],
+                lambda part: l3[h, 1, part, :],
+                lambda part: l3[h, 2, part, :],
+                lambda part: l3[h, 3, part, :],
+                lambda part: og[part, h * half : (h + 1) * half],
+            ],
+        )
+    for copy in started:
+        copy.wait_send()
+
+
+def per_device_tokens(
+    output_grad,
+    gate_values,
+    expert_ids,
+    pre_gate,
+    pre_up,
+    w_gate,
+    w_up,
+    w_down,
+    visual,
+    visual_rows,
+):
+    tok, width = output_grad.shape
+    half = width // 2
+    experts = lax.axis_size("expert")
+    capacity, hid = pre_gate.shape[2:]
+    named = expert_ids[:, :, None] == jnp.arange(experts, dtype=jnp.int32)
+    weight = jnp.sum(jnp.where(named, gate_values[:, :, None], 0.0), axis=1)
+    here = jnp.any(named, axis=1)
+    count = here.astype(jnp.int32)
+    position = jnp.where(here, jnp.cumsum(count, axis=0) - count, -1).astype(jnp.float32)
+    info = jnp.stack([weight.T, position.T], axis=1)
+    info = lax.all_to_all(info, "expert", split_axis=0, concat_axis=0, tiled=True)
+    info = jnp.transpose(info, (0, 2, 1))
+    bf, dma = jnp.bfloat16, pltpu.SemaphoreType.DMA
+    rows = 4 * tok
+    input_grad = pl.pallas_call(
+        expert_kernel,
+        out_shape=jax.ShapeDtypeStruct((tok, width), bf),
+        in_specs=[pl.BlockSpec(memory_space=pltpu.VMEM)] * 7,
+        out_specs=pl.BlockSpec(memory_space=pltpu.VMEM),
+        scratch_shapes=[
+            pltpu.VMEM((2, 4, 4, tok, half), bf),
+            pltpu.VMEM((2, 4, 4, tok, half), bf),
+            pltpu.VMEM((4, 4, tok, hid), bf),
+            pltpu.VMEM((4, 4, tok, hid), bf),
+            pltpu.VMEM((2, rows, hid), jnp.float32),
+            pltpu.VMEM((4, rows, hid), bf),
+            pltpu.VMEM((4, rows, hid), bf),
+            pltpu.VMEM((rows, hid), bf),
+            pltpu.VMEM((rows, hid), bf),
+            pltpu.VMEM((2, 2, 4, tok, half), bf),
+            pltpu.VMEM((2, 4, tok, half), bf),
+            pltpu.VMEM((2, 4, tok, half), bf),
+        ]
+        + [dma((4, 2))] * 8
+        + [dma((4,))] * 2
+        + [dma((4, 4))] * 2
+        + [dma((2, 4))] * 4,
+        compiler_params=pltpu.CompilerParams(
+            collective_id=0, has_side_effects=True, vmem_limit_bytes=63 * 1024 * 1024
+        ),
+        cost_estimate=pl.CostEstimate(
+            flops=6 * 4 * rows * width * hid, bytes_accessed=20 * 1024 * 1024, transcendentals=0
+        ),
+    )(
+        output_grad, info,
+        pre_gate[0].reshape(4, 4, capacity, hid), pre_up[0].reshape(4, 4, capacity, hid),
+        w_gate[0], w_up[0], w_down[0],
+    )
+    return (input_grad, projector(input_grad, visual, visual_rows))
+
+
+def projector(input_grad, visual, visual_rows):
+    visual_grad = input_grad[visual_rows]
+    features = lax.all_to_all(visual, "expert", split_axis=1, concat_axis=0, tiled=True)
+    return jnp.einsum(
+        "rv,rd->vd",
+        features,
+        lax.all_gather(visual_grad, "expert", axis=0, tiled=True),
+        preferred_element_type=jnp.float32,
+    )
+
+
 def solution(mesh):
+    per_rank = per_device_tokens if mesh.shape["expert"] == 16 else per_device
     in_specs = (
         P(("groups", "expert"), "tower"),
         P(("groups", "expert"), None),
@@ -89,5 +406,5 @@
     )
     out_specs = (P(("groups", "expert"), "tower"), P(("groups", "expert"), "tower"))
     return jax.shard_map(
-        per_device, mesh=mesh, in_specs=in_specs, out_specs=out_specs, check_vma=False
-    )
+        per_rank, mesh=mesh, in_specs=in_specs, out_specs=out_specs, check_vma=False
+    )

time: 537 us -> 271 us (0.50)
  blocking collectives: 211 us -> 15.6 us
  Pallas kernels: 0 us -> 172 us
  waiting for transfers between devices: 211 us -> 48.9 us
  matrix products: 39 us -> 2.38 us
  local copies, waits for them, and re-layouts: 42.3 us -> 6.6 us
  other arithmetic: 12.9 us -> 2.28 us
    all_to_all x2 -> x1, blocking collectives: 211 us -> 15.6 us  [projector(): lax.all_to_all(visual, 'expert', split_axis=1, concat_axis=0, tiled=True)]
    pallas_call x0 -> x1, Pallas kernels: none -> 172 us  [per_device_tokens(): pl.pallas_call(expert_kernel, out_shape=jax.ShapeDtypeStruct((tok, width)...]
    all_to_all x1, waiting for transfers between devices: 139 us -> 6.61 us  [per_device_tokens(): lax.all_to_all(info, 'expert', split_axis=0, concat_axis=0, tiled=True)]
    dot_general x4 -> x1, matrix products: 39 us -> 2.38 us  [projector(): jnp.einsum('rv,rd->vd', features, lax.all_gather(visual_grad, 'expert', a...]
    psum x1 -> x0, waiting for transfers between devices: 29 us -> none  [per_device(): summed = lax.psum(partial_value, 'tower')]
    scatter x1 -> x0, local copies, waits for them, and re-layouts: 24.9 us -> none  [per_device(): outgoing = jnp.zeros((expert_count * capacity, half_width), jnp.bfloat16)...]
    gather x2 -> x1, local copies, waits for them, and re-layouts: 15.4 us -> 2.4 us  [projector(): visual_grad = input_grad[visual_rows]]
    reduce_sum x2 -> x1, other arithmetic: 6.6 us -> 0.72 us  [per_device_tokens(): weight = jnp.sum(jnp.where(named, gate_values[:, :, None], 0.0), axis=1)]
  transfers between devices with their start and end apart: 3 -> 2, of which waited for: 3 -> 2; matrix products, arithmetic and copies ran while one was open for 0% -> 0% of each run, Pallas kernels for 0% -> 0%
where the time goes in v2:
time: 271 us
  Pallas kernels  172 us (63%)
  waiting for transfers between devices  48.9 us (18%)
  blocking collectives  15.6 us (6%)
  between operations  14.1 us (5%)
  starting transfers between devices  8.35 us (3%)
  local copies, waits for them, and re-layouts  6.6 us (2%)
    pallas_call x1, Pallas kernels, per_device_tokens(): pl.pallas_call(expert_kernel, out_shape=jax.ShapeDtypeStruct((tok, width)...  172 us
    all_gather x1, waiting for transfers between devices, projector(): lax.all_gather(visual_grad, 'expert', axis=0, tiled=True)  42.3 us
    all_to_all x1, blocking collectives, projector(): lax.all_to_all(visual, 'expert', split_axis=1, concat_axis=0, tiled=True)  15.6 us
    all_to_all x1, starting transfers between devices, per_device_tokens(): lax.all_to_all(info, 'expert', split_axis=0, concat_axis=0, tiled=True)  8.31 us
    all_to_all x1, waiting for transfers between devices, per_device_tokens(): lax.all_to_all(info, 'expert', split_axis=0, concat_axis=0, tiled=True)  6.61 us
  transfers between devices with their start and end apart: 2, of which 2 were waited for; matrix products, arithmetic and copies ran while one was open for 0% of the time, Pallas kernels for 0%

profile of v2, /device:TPU:0, one launch (start us, length us, event | category | flops | bytes accessed | tf_op | source)
XLA Modules:
  0.0 270.6 jit_solution(7411172355684909192)
XLA Ops:
  7.2 0.7 fusion
  7.9 0.7 select_reduce_fusion
  8.6 0.1 copy.34
  8.7 0.2 reduce_window_sum.13
  8.9 0.1 copy.35
  8.9 0.6 copy.36
  9.6 8.3 %all-to-all-start = ((f32[16,2,128]{2,1,0:T(2,128)}), f32[16,2,128]{2,1,0:T(2,128)S(1)}, u32[]{:S(2)}, u32[]{:S(2)}) async-start(f32[16,2,128]{2,1,0:T(2,128)} %copy.36), calls=%async_computation | async-start | bytes 32768 | tf_op jit(solution)/shard_map/all_to_all | solution.py:341
  17.9 0.0 all-gather.3.cloned.1.call-start
  17.9 0.7 compare_select_fusion
  18.6 6.6 %all-to-all-done = f32[16,2,128]{2,1,0:T(2,128)S(1)} async-done(((f32[16,2,128]{2,1,0:T(2,128)}), f32[16,2,128]{2,1,0:T(2,128)S(1)}, u32[]{:S(2)}, u32[]{:S(2)}) %all-to-all-start) | async-done | bytes 16416 | tf_op jit(solution)/shard_map/all_to_all | solution.py:341
  25.2 1.4 copy.37
  26.6 0.0 copy-start
  26.6 172.4 %shard_map.113 = bf16[128,2048]{1,0:T(8,128)(2,1)} custom-call(bf16[128,2048]{1,0:T(8,128)(2,1)} %og.1, f32[16,128,2]{2,1,0:T(8,128)} %bitcast.28, bf16[4,4,112,768]{3,2,1,0:T(8,128)(2,1)} %bitcast.34, bf16[4,4,112,768]{3,2,1,0:T(8,128)(2,1)} %bitcast.35, bf16[2048,768]{1,0:T(8,128)(2,1)} %bitcast.31, bf16[2048,768]{1,0:T(8,128)(2,1)} %bitcast.32, ...), custom_call_target="tpu_custom_call" | custom-call | flops 19327352832 | bytes 20971520 | tf_op jit(solution)/shard_map/pallas_call | solution.py:345
  199.0 2.4 gather_fusion
  201.4 0.0 all-gather.3.cloned.1.call-update
  201.4 0.0 copy-done
  201.4 0.1 all_to_all.18
  201.6 15.6 %all_to_all.24 = bf16[16,16,72]{2,0,1:T(8,128)(2,1)S(1)} all-to-all(bf16[16,16,72]{2,0,1:T(8,128)(2,1)S(1)} %copy.38), channel_id=1, replica_groups=mesh['groups'=1,'expert'=16,'tower'=2] {'expert'}, dimensions={1} | all-to-all | bytes 73728 | tf_op jit(solution)/shard_map/all_to_all | solution.py:384
  217.2 42.3 %all-gather.3.cloned.1.call-done = bf16[256,2048]{1,0:T(8,128)(2,1)} async-done(((bf16[16,2048]{1,0:T(8,128)(2,1)}), bf16[256,2048]{1,0:T(8,128)(2,1)}) %all-gather.3.cloned.1.call-update) | async-done | bytes 1048592 | tf_op jit(solution)/shard_map/all_gather | solution.py:388
  259.5 2.4 convolution_bitcast_fusion
  261.9 1.9 copy.40
  (5 shorter events, 0.0 us)
Async XLA Ops:
  9.6 15.7 %all-to-all-start = ((f32[16,2,128]{2,1,0:T(2,128)}), f32[16,2,128]{2,1,0:T(2,128)S(1)}, u32[]{:S(2)}, u32[]{:S(2)}) async-start(f32[16,2,128]{2,1,0:T(2,128)} %copy.36), calls=%async_computation | async-start | bytes 32768 | tf_op jit(solution)/shard_map/all_to_all | solution.py:341
  17.9 241.6 %all-gather.3.cloned.1.call-start = ((), (), s32[]{:S(2)}) async-start(), calls=%async_computation.2 | async-start | bytes 1114112 | tf_op jit(solution)/shard_map/all_gather | solution.py:388
  26.6 174.8 %copy-start = (bf16[16,1152]{1,0:T(8,128)(2,1)S(1)}, bf16[16,1152]{1,0:T(8,128)(2,1)}, u32[]{:S(2)}) copy-start(bf16[16,1152]{1,0:T(8,128)(2,1)} %param.18) | copy-start | bytes 110596
Sparse Core Ops, SparseCore 0:
  201.5 57.9 all-gather.2

commit v3 on v2

--- a/solution.py
+++ b/solution.py
@@ -77,9 +77,10 @@
 
 
 def expert_kernel(
-    og, info, pg, pu, wg, wu, wd, out,
+    og, info, pg, pu, wg, wu, wd, visual, vrows, out, vgrad_out, vis_out,
     held, contrib, gate_tok, up_tok, own_sum, half_out, half_in, grad_g, grad_u, l1, l2, l3,
     zs, zr, xs, xr, ys, yr, fs, fr, hs, hr, s1, r1, s2, r2, s3, r3,
+    vis, vgrad, vs, vr, gs, gr,
 ):
     zl, tok, half = held.shape[2:]
     hid = wd.shape[0]
@@ -110,6 +111,7 @@
         pl.semaphore_signal(barrier, inc=1, device_id=device, device_id_type=pl.DeviceIdType.MESH)
     for h in range(2):
         held[h, q, z] = og[:, h * half : (h + 1) * half]
+    vis[q, z] = visual[...]
     pl.semaphore_wait(barrier, 6)
 
     started = []
@@ -126,6 +128,28 @@
     def to_y(k, h):
         block = held.at[h, q, zfrom[k]]
         return go(remote(block, block, ys.at[k, h], yr.at[k, h], yn))
+
+    def along_z(buf, ss, rs):
+        block = buf.at[q, z]
+        return [go(remote(block, block, ss.at[k - 1], rs.at[k - 1], zdev[k])) for k in (1, 2, 3)]
+
+    def across(buf, ss, rs, copies):
+        for copy in copies:
+            copy.wait_recv()
+        line = buf.at[q]
+        return [
+            go(remote(line, line, ss.at[3], rs.at[3], xn)),
+            go(remote(line, line, ss.at[4], rs.at[4], yn)),
+        ]
+
+    def diagonal(buf, ss, rs, copies):
+        for copy in copies:
+            copy.wait_recv()
+        low, high = buf.at[qx, pl.ds(0, 2)], buf.at[qy, pl.ds(2, 2)]
+        return [
+            go(remote(low, low, ss.at[5], rs.at[5], yn)),
+            go(remote(high, high, ss.at[6], rs.at[6], xn)),
+        ]
 
     zc, xc, yc, fc = {}, {}, {}, {}
 
@@ -146,6 +170,7 @@
         go(zc[k, 0])
         go(zc[k, 1])
     xc[0, 1], yc[0, 0] = to_x(0, 1), to_y(0, 0)
+    vc = along_z(vis, vs, vr)
 
     @pl.loop(0, 4)
     def _(zi):
@@ -229,6 +254,7 @@
                 )
             )
 
+    vc = across(vis, vs, vr, vc)
     hidden(0, q)
     forward(2)
     for k in range(4):
@@ -243,6 +269,7 @@
     for k in range(4):
         fc[k, 0].wait_recv()
         fc[k, 1].wait_recv()
+    vc = diagonal(vis, vs, vr, vc)
     hidden(3, qd)
     finish(2, qy)
     first(0, 0, qy, yn)
@@ -312,6 +339,19 @@
                 lambda part: og[part, h * half : (h + 1) * half],
             ],
         )
+    choice = vrows[...] == lax.broadcasted_iota(jnp.int32, (vrows.shape[0], tok), 1)
+    choice = jnp.where(choice, 1.0, 0.0).astype(jnp.bfloat16)
+    for c in range(0, 2 * half, 512):
+        vgrad[q, z, :, c : c + 512] = jnp.dot(
+            choice, out[:, c : c + 512], preferred_element_type=jnp.float32
+        ).astype(jnp.bfloat16)
+    gc = across(vgrad, gs, gr, along_z(vgrad, gs, gr))
+    for copy in vc:
+        copy.wait_recv()
+    vis_out[...] = vis[...]
+    for copy in diagonal(vgrad, gs, gr, gc):
+        copy.wait_recv()
+    vgrad_out[...] = vgrad[...]
     for copy in started:
         copy.wait_send()
 
@@ -342,11 +382,16 @@
     info = jnp.transpose(info, (0, 2, 1))
     bf, dma = jnp.bfloat16, pltpu.SemaphoreType.DMA
     rows = 4 * tok
-    input_grad = pl.pallas_call(
+    vis_rows, vis_width = visual.shape
+    input_grad, vgrad, vis = pl.pallas_call(
         expert_kernel,
-        out_shape=jax.ShapeDtypeStruct((tok, width), bf),
-        in_specs=[pl.BlockSpec(memory_space=pltpu.VMEM)] * 7,
-        out_specs=pl.BlockSpec(memory_space=pltpu.VMEM),
+        out_shape=(
+            jax.ShapeDtypeStruct((tok, width), bf),
+            jax.ShapeDtypeStruct((4, 4, vis_rows, width), bf),
+            jax.ShapeDtypeStruct((4, 4, vis_rows, vis_width), bf),
+        ),
+        in_specs=[pl.BlockSpec(memory_space=pltpu.VMEM)] * 9,
+        out_specs=(pl.BlockSpec(memory_space=pltpu.VMEM),) * 3,
         scratch_shapes=[
             pltpu.VMEM((2, 4, 4, tok, half), bf),
             pltpu.VMEM((2, 4, 4, tok, half), bf),
@@ -364,7 +409,12 @@
         + [dma((4, 2))] * 8
         + [dma((4,))] * 2
         + [dma((4, 4))] * 2
-        + [dma((2, 4))] * 4,
+        + [dma((2, 4))] * 4
+        + [
+            pltpu.VMEM((4, 4, vis_rows, vis_width), bf),
+            pltpu.VMEM((4, 4, vis_rows, width), bf),
+        ]
+        + [dma((7,))] * 4,
         compiler_params=pltpu.CompilerParams(
             collective_id=0, has_side_effects=True, vmem_limit_bytes=63 * 1024 * 1024
         ),
@@ -374,20 +424,16 @@
     )(
         output_grad, info,
         pre_gate[0].reshape(4, 4, capacity, hid), pre_up[0].reshape(4, 4, capacity, hid),
-        w_gate[0], w_up[0], w_down[0],
-    )
-    return (input_grad, projector(input_grad, visual, visual_rows))
-
-
-def projector(input_grad, visual, visual_rows):
-    visual_grad = input_grad[visual_rows]
-    features = lax.all_to_all(visual, "expert", split_axis=1, concat_axis=0, tiled=True)
-    return jnp.einsum(
-        "rv,rd->vd",
-        features,
-        lax.all_gather(visual_grad, "expert", axis=0, tiled=True),
-        preferred_element_type=jnp.float32,
-    )
+        w_gate[0], w_up[0], w_down[0], visual, visual_rows[:, None],
+    )
+    share = vis_width // experts
+    features = lax.dynamic_slice_in_dim(
+        vis.reshape(-1, vis_width), lax.axis_index("expert") * share, share, axis=1
+    )
+    projector_grad = jnp.einsum(
+        "rv,rd->vd", features, vgrad.reshape(-1, width), preferred_element_type=jnp.float32
+    )
+    return (input_grad, projector_grad)
 
 
 def solution(mesh):

time: 271 us -> 222 us (0.82)
  waiting for transfers between devices: 48.9 us -> 5.99 us
  Pallas kernels: 172 us -> 197 us
  blocking collectives: 15.6 us -> 0 us
  between operations: 14.1 us -> 0.67 us
    all_gather x1 -> x0, waiting for transfers between devices: 42.3 us -> none  [projector(): lax.all_gather(visual_grad, 'expert', axis=0, tiled=True)]
    pallas_call x1, Pallas kernels: 172 us -> 197 us  [per_device_tokens(): pl.pallas_call(expert_kernel, out_shape=(jax.ShapeDtypeStruct((tok, width...]
    all_to_all x1 -> x0, blocking collectives: 15.6 us -> none  [projector(): lax.all_to_all(visual, 'expert', split_axis=1, concat_axis=0, tiled=True)]
  transfers between devices with their start and end apart: 2 -> 1, of which waited for: 2 -> 1; matrix products, arithmetic and copies ran while one was open for 0% -> 1% of each run, Pallas kernels for 0% -> 0%
where the time goes in v3:
time: 222 us; the launch traced here: 221 us
  Pallas kernels  197 us (89%)
  starting transfers between devices  8.31 us (4%)
  waiting for transfers between devices  5.99 us (3%)
  local copies, waits for them, and re-layouts  5.34 us (2%)
  matrix products  2.53 us (1%)
    pallas_call x1, Pallas kernels, per_device_tokens(): pl.pallas_call(expert_kernel, out_shape=(jax.ShapeDtypeStruct((tok, width...  197 us
    all_to_all x1, starting transfers between devices, per_device_tokens(): lax.all_to_all(info, 'expert', split_axis=0, concat_axis=0, tiled=True)  8.31 us
    all_to_all x1, waiting for transfers between devices, per_device_tokens(): lax.all_to_all(info, 'expert', split_axis=0, concat_axis=0, tiled=True)  5.99 us
  transfers between devices with their start and end apart: 1, of which 1 were waited for; matrix products, arithmetic and copies ran while one was open for 1% of the time, Pallas kernels for 0%

profile of v3, /device:TPU:0, one launch (start us, length us, event | category | flops | bytes accessed | tf_op | source)
XLA Modules:
  0.0 221.4 jit_solution(17437326557218168950)
XLA Ops:
  0.6 0.7 fusion.2
  1.3 0.1 copy.35
  1.4 0.2 reduce_window_sum.13
  1.6 0.1 copy.36
  1.7 0.7 select_reduce_fusion
  2.4 0.6 copy.37
  3.0 8.3 %all-to-all-start = ((f32[16,2,128]{2,1,0:T(2,128)}), f32[16,2,128]{2,1,0:T(2,128)S(1)}, u32[]{:S(2)}, u32[]{:S(2)}) async-start(f32[16,2,128]{2,1,0:T(2,128)} %copy.37), calls=%async_computation | async-start | bytes 32768 | tf_op jit(solution)/shard_map/all_to_all | solution.py:381
  11.4 1.3 copy.39.vrows
  12.7 6.0 %all-to-all-done = f32[16,2,128]{2,1,0:T(2,128)S(1)} async-done(((f32[16,2,128]{2,1,0:T(2,128)}), f32[16,2,128]{2,1,0:T(2,128)S(1)}, u32[]{:S(2)}, u32[]{:S(2)}) %all-to-all-start) | async-done | bytes 16416 | tf_op jit(solution)/shard_map/all_to_all | solution.py:381
  18.7 1.4 copy.38
  20.1 196.9 %shard_map.113 = (bf16[128,2048]{1,0:T(8,128)(2,1)}, bf16[4,4,16,2048]{3,2,1,0:T(8,128)(2,1)}, bf16[4,4,16,1152]{3,2,1,0:T(8,128)(2,1)}) custom-call(bf16[128,2048]{1,0:T(8,128)(2,1)} %og.1, f32[16,128,2]{2,1,0:T(8,128)} %bitcast.26, bf16[4,4,112,768]{3,2,1,0:T(8,128)(2,1)} %bitcast.33, bf16[4,4,112,768]{3,2,1,0:T(8,128)(2,1)} %bitcast.34, ...), custom_call_target="tpu_custom_call" | custom-call | flops 19327352832 | bytes 20971520 | tf_op jit(solution)/shard_map/pallas_call | solution.py:386
  216.9 2.5 %fusion = f32[72,2048]{1,0:T(8,128)} fusion(bf16[256,2048]{1,0:T(8,128)(2,1)} %bitcast.25, bf16[256,1152]{1,0:T(8,128)(2,1)} %bitcast.28, s32[]{:T(128)S(6)} %select_n.14), kind=kOutput, calls=%fused_computation | convolution fusion | flops 75497472 | bytes 1703940 | tf_op jit(solution)/shard_map/rv,rd->vd/dot_general | solution.py:433
  219.5 1.9 copy.41
  (3 shorter events, 0.0 us)
Async XLA Ops:
  3.0 15.7 %all-to-all-start = ((f32[16,2,128]{2,1,0:T(2,128)}), f32[16,2,128]{2,1,0:T(2,128)S(1)}, u32[]{:S(2)}, u32[]{:S(2)}) async-start(f32[16,2,128]{2,1,0:T(2,128)} %copy.37), calls=%async_computation | async-start | bytes 32768 | tf_op jit(solution)/shard_map/all_to_all | solution.py:381

commit v4 on v3

--- a/solution.py
+++ b/solution.py
@@ -77,10 +77,10 @@
 
 
 def expert_kernel(
-    og, info, pg, pu, wg, wu, wd, visual, vrows, out, vgrad_out, vis_out,
+    og, info_own, pg, pu, wg, wu, wd, visual, vrows, out, vgrad_out, vis_out,
     held, contrib, gate_tok, up_tok, own_sum, half_out, half_in, grad_g, grad_u, l1, l2, l3,
     zs, zr, xs, xr, ys, yr, fs, fr, hs, hr, s1, r1, s2, r2, s3, r3,
-    vis, vgrad, vs, vr, gs, gr,
+    vis, vgrad, vs, vr, gs, gr, info, ns, nr,
 ):
     zl, tok, half = held.shape[2:]
     hid = wd.shape[0]
@@ -112,6 +112,7 @@
     for h in range(2):
         held[h, q, z] = og[:, h * half : (h + 1) * half]
     vis[q, z] = visual[...]
+    info[q, z] = info_own[...]
     pl.semaphore_wait(barrier, 6)
 
     started = []
@@ -165,24 +166,18 @@
         for h in range(2):
             block = held.at[h, q, z]
             zc[k, h] = remote(block, block, zs.at[k, h], zr.at[k, h], zdev[k])
+    nc = along_z(info, ns, nr)
     xc[0, 0], yc[0, 1] = to_x(0, 0), to_y(0, 1)
     for k in (1, 3, 2):
         go(zc[k, 0])
         go(zc[k, 1])
     xc[0, 1], yc[0, 0] = to_x(0, 1), to_y(0, 0)
     vc = along_z(vis, vs, vr)
-
-    @pl.loop(0, 4)
-    def _(zi):
-        @pl.loop(0, 4)
-        def _(qi):
-            place = info[zi * 4 + qi, :, 1:2]
-            slot = lax.broadcasted_iota(jnp.int32, (tok, cap), 1).astype(jnp.float32)
-            spread = jnp.where(place == slot, 1.0, 0.0).astype(jnp.bfloat16)
-            for pre, dest in ((pg, gate_tok), (pu, up_tok)):
-                dest[qi, zi] = jnp.dot(
-                    spread, pre[zi, qi], preferred_element_type=jnp.float32
-                ).astype(jnp.bfloat16)
+    nc = across(info, ns, nr, nc)
+
+    def pick(block, lane):
+        lanes = lax.broadcasted_iota(jnp.int32, block.shape, 1)
+        return jnp.sum(jnp.where(lanes == lane, block, 0.0), axis=1, keepdims=True)
 
     done = None
     for k in (1, 3, 2):
@@ -192,6 +187,8 @@
         yc[k, 1] = to_y(k, 1)
         xc[k, 1], yc[k, 0] = to_x(k, 1), to_y(k, 0)
         forward(0 if done is None else done)
+        if done is None:
+            nc = diagonal(info, ns, nr, nc)
         done = k
 
     hc = []
@@ -220,7 +217,7 @@
         def _(zi):
             part = pl.ds(pl.multiple_of(zi * tok, tok), tok)
             summed = own_sum[g % 2, part, :] + half_in[g, part, :].astype(jnp.float32)
-            summed = summed * info[zi * 4 + qq, :, 0:1]
+            summed = summed * pick(info[qq, zi], me)
             gate = gate_tok[qq, zi].astype(jnp.float32)
             up = up_tok[qq, zi].astype(jnp.float32)
             sig = jax.nn.sigmoid(gate)
@@ -255,6 +252,21 @@
             )
 
     vc = across(vis, vs, vr, vc)
+    for copy in nc:
+        copy.wait_recv()
+
+    @pl.loop(0, 4)
+    def _(zi):
+        @pl.loop(0, 4)
+        def _(qi):
+            place = pick(info[qi, zi], 16 + me)
+            slot = lax.broadcasted_iota(jnp.int32, (tok, cap), 1).astype(jnp.float32)
+            spread = jnp.where(place == slot, 1.0, 0.0).astype(jnp.bfloat16)
+            for pre, dest in ((pg, gate_tok), (pu, up_tok)):
+                dest[qi, zi] = jnp.dot(
+                    spread, pre[zi, qi], preferred_element_type=jnp.float32
+                ).astype(jnp.bfloat16)
+
     hidden(0, q)
     forward(2)
     for k in range(4):
@@ -377,9 +389,8 @@
     here = jnp.any(named, axis=1)
     count = here.astype(jnp.int32)
     position = jnp.where(here, jnp.cumsum(count, axis=0) - count, -1).astype(jnp.float32)
-    info = jnp.stack([weight.T, position.T], axis=1)
-    info = lax.all_to_all(info, "expert", split_axis=0, concat_axis=0, tiled=True)
-    info = jnp.transpose(info, (0, 2, 1))
+    info = jnp.concatenate([weight, position], axis=1)
+    info = jnp.pad(info, ((0, 0), (0, 128 - 2 * experts)))
     bf, dma = jnp.bfloat16, pltpu.SemaphoreType.DMA
     rows = 4 * tok
     vis_rows, vis_width = visual.shape
@@ -414,7 +425,9 @@
             pltpu.VMEM((4, 4, vis_rows, vis_width), bf),
             pltpu.VMEM((4, 4, vis_rows, width), bf),
         ]
-        + [dma((7,))] * 4,
+        + [dma((7,))] * 4
+        + [pltpu.VMEM((4, 4, tok, 128), jnp.float32)]
+        + [dma((7,))] * 2,
         compiler_params=pltpu.CompilerParams(
             collective_id=0, has_side_effects=True, vmem_limit_bytes=63 * 1024 * 1024
         ),

time: 222 us -> 223 us (level)
  Pallas kernels: 197 us -> 214 us
  starting transfers between devices: 8.31 us -> 0 us
  waiting for transfers between devices: 5.99 us -> 0 us
    pallas_call x1, Pallas kernels: 197 us -> 214 us  [per_device_tokens(): pl.pallas_call(expert_kernel, out_shape=(jax.ShapeDtypeStruct((tok, width...]
    all_to_all x1 -> x0, starting transfers between devices: 8.31 us -> none  [per_device_tokens(): lax.all_to_all(info, 'expert', split_axis=0, concat_axis=0, tiled=True)]
    all_to_all x1 -> x0, waiting for transfers between devices: 5.99 us -> none  [per_device_tokens(): lax.all_to_all(info, 'expert', split_axis=0, concat_axis=0, tiled=True)]
  transfers between devices with their start and end apart: 1 -> 0, of which waited for: 1 -> 0; matrix products, arithmetic and copies ran while one was open for 1% -> 0% of each run, Pallas kernels for 0% -> 0%
where the time goes in v4:
time: 223 us
  Pallas kernels  214 us (96%)
  local copies, waits for them, and re-layouts  4.14 us (2%)
  matrix products  2.53 us (1%)
    pallas_call x1, Pallas kernels, per_device_tokens(): pl.pallas_call(expert_kernel, out_shape=(jax.ShapeDtypeStruct((tok, width...  214 us

profile of v4, /device:TPU:0, one launch (start us, length us, event | category | flops | bytes accessed | tf_op | source)
XLA Modules:
  0.0 222.5 jit_solution(11778458684356977678)
XLA Ops:
  0.6 0.7 fusion.2
  1.3 0.7 select_reduce_fusion
  2.1 1.3 copy.24.vrows
  3.4 0.1 copy.21
  3.5 0.2 reduce_window_sum.11
  3.7 0.1 copy.22
  3.8 0.1 copy.23
  3.9 0.6 pad.4.info_own
  4.5 213.5 %shard_map.113 = (bf16[128,2048]{1,0:T(8,128)(2,1)}, bf16[4,4,16,2048]{3,2,1,0:T(8,128)(2,1)}, bf16[4,4,16,1152]{3,2,1,0:T(8,128)(2,1)}) custom-call(bf16[128,2048]{1,0:T(8,128)(2,1)} %og.1, f32[128,128]{1,0:T(8,128)} %pad.4.info_own, bf16[4,4,112,768]{3,2,1,0:T(8,128)(2,1)} %bitcast.15, bf16[4,4,112,768]{3,2,1,0:T(8,128)(2,1)} %bitcast.16, ...), custom_call_target="tpu_custom_call" | custom-call | flops 19327352832 | bytes 20971520 | tf_op jit(solution)/shard_map/pallas_call | solution.py:397
  218.1 2.5 %fusion = f32[72,2048]{1,0:T(8,128)} fusion(bf16[256,2048]{1,0:T(8,128)(2,1)} %bitcast.9, bf16[256,1152]{1,0:T(8,128)(2,1)} %bitcast.10, s32[]{:T(128)S(6)} %select_n.13), kind=kOutput, calls=%fused_computation | convolution fusion | flops 75497472 | bytes 1703940 | tf_op jit(solution)/shard_map/rv,rd->vd/dot_general | solution.py:446
  220.6 1.9 copy.26
  (4 shorter events, 0.0 us)
